TPU v7x, 32 devices: a whole 2x2x4 slice. The times are simulated.
32 devices in a mesh: req: 16 (over z, y, x), tp: 2 (over core).
Axes of the slice: x: 2, y: 2, z: 4, core: 2. Of those that a mesh axis runs over, the one named last changes fastest.
Arguments:
- residual: bfloat16 [512, 2048], P('req'), may hold values from -6 to 6
- fresh_qkv: bfloat16 [512, 3, 2048], P('req', None, 'tp'), may hold values from -32 to 32
- kv_cache: bfloat16 [512, 24, 2, 2048], P('req', None, None, 'tp'), may hold values from -32 to 32
- cache_len: int32 [512], P('req'), may hold values from 2 to 24, as said below
- out_proj: bfloat16 [2048, 2048], P('tp'), may hold values from -0.125 to 0.125
- norm_gain: float32 [2048], replicated, may hold values from 0.1 to 1.9
- router_weight: float32 [2048, 16], replicated, may hold values from -7.9549513 to 7.9549513
- expert_ids: int32 [512, 8], P('req'), may hold values from 0 to 15, all different within a row; in each aligned block of 32 rows (0 to 31, 32 to 63, ...) at most 32 rows name the same one
- gate_up: bfloat16 [16, 2048, 2, 1024], P('req', None, None, 'tp'), may hold values from -0.125 to 0.125
- down_proj: bfloat16 [16, 1024, 2048], P('req', 'tp'), may hold values from -0.1875 to 0.1875
Outputs:
- layer_out: bfloat16 [512, 2048], P('req', 'tp')
Inputs may be any that keep to these rules, and one draw needn't show every extreme that they name: `expert_ids`: each row names 8 different experts; among the 32 rows of one device no expert is named by more than 32 rows, and some device reaches 32. `cache_len`: some request uses all 24 positions.
All inputs are finite; a program needn't handle non-finite values.
Results may differ from a plain program's by a relative error of at most 0.018.
Values may be sent and summed in bfloat16 or wider, within the bound.
A program may use at most 128 MiB of HBM per device.

v0:
```python
import jax
import jax.numpy as jnp
from jax import lax
from jax.sharding import PartitionSpec as P

HD = 128
TOP = 8


def rms_normed(hidden_in, gain):
    values = hidden_in.astype(jnp.float32)
    scale_inv = lax.rsqrt(jnp.mean(values * values, axis=-1, keepdims=True) + 1e-05)
    return (values * scale_inv * gain).astype(jnp.bfloat16)


def expert_part(slots_in, gate_up, down_proj):
    layout = slots_in.shape
    flat_in = slots_in.reshape(-1, layout[-1])
    units_here = down_proj.shape[1]
    both = jnp.dot(
        flat_in, gate_up[0].reshape(layout[-1], 2 * units_here), preferred_element_type=jnp.float32
    )
    both = both.reshape(-1, 2, units_here)
    inner = (jax.nn.silu(both[:, 0]) * both[:, 1]).astype(jnp.bfloat16)
    result = jnp.dot(inner, down_proj[0], preferred_element_type=jnp.float32)
    return result.reshape(layout[:-1] + (down_proj.shape[2],))


def send_back(results):
    return lax.all_to_all(results, "req", split_axis=0, concat_axis=0, tiled=True)


def local(
    residual,
    fresh_qkv,
    kv_cache,
    cache_len,
    out_proj,
    norm_gain,
    router_weight,
    expert_ids,
    gate_up,
    down_proj,
):
    requests = residual.shape[0]
    tp_place = lax.axis_index("tp")
    experts = lax.axis_size("req")
    capacity = 2 * requests * TOP // experts
    local_heads = fresh_qkv.shape[2] // HD
    ctx_len = kv_cache.shape[1]
    queries = fresh_qkv[:, 0].reshape(requests, local_heads, HD)
    new_keys = fresh_qkv[:, 1].reshape(requests, local_heads, HD)
    new_values = fresh_qkv[:, 2].reshape(requests, local_heads, HD)
    cache_keys = kv_cache[:, :, 0].reshape(requests, ctx_len, local_heads, HD)
    cache_values = kv_cache[:, :, 1].reshape(requests, ctx_len, local_heads, HD)
    factor = HD ** (-0.5)
    scores = (
        jnp.einsum("nhd,nchd->nhc", queries, cache_keys, preferred_element_type=jnp.float32)
        * factor
    )
    own_score = (
        jnp.einsum("nhd,nhd->nh", queries, new_keys, preferred_element_type=jnp.float32) * factor
    )
    valid = (jnp.arange(ctx_len, dtype=jnp.int32)[None, :] < cache_len[:, None])[:, None, :]
    masked = jnp.where(valid, scores, -jnp.inf)
    top_score = jnp.maximum(jnp.max(masked, axis=-1), own_score)
    expos = jnp.where(valid, jnp.exp(masked - top_score[..., None]), 0.0)
    own_expo = jnp.exp(own_score - top_score)
    total = jnp.sum(expos, axis=-1) + own_expo
    weights = (expos / total[..., None]).astype(jnp.bfloat16)
    own_weight = (own_expo / total).astype(jnp.bfloat16)
    mixed = jnp.einsum("nhc,nchd->nhd", weights, cache_values, preferred_element_type=jnp.float32)
    mixed = mixed + own_weight.astype(jnp.float32)[..., None] * new_values.astype(jnp.float32)
    attended = mixed.astype(jnp.bfloat16).reshape(requests, local_heads * HD)
    partial_value = jnp.dot(attended, out_proj, preferred_element_type=jnp.float32)
    summed = lax.psum(partial_value, "tp")
    hidden = (residual.astype(jnp.float32) + summed).astype(jnp.bfloat16)
    normed = rms_normed(hidden, norm_gain)
    logits = jnp.dot(normed.astype(jnp.float32), router_weight, precision=lax.Precision.HIGHEST)
    chosen = jnp.take_along_axis(logits, expert_ids, axis=1)
    gate_vals = jax.nn.softmax(chosen, axis=-1)
    flat_ids = expert_ids.reshape(-1)
    onehot = (flat_ids[:, None] == jnp.arange(experts, dtype=jnp.int32)[None, :]).astype(jnp.int32)
    running = jnp.cumsum(onehot, axis=0)
    slot_index = jnp.sum(running * onehot, axis=1) - 1
    position = flat_ids * capacity + slot_index
    selector = (
        position[None, :] == jnp.arange(experts * capacity, dtype=jnp.int32)[:, None]
    ).astype(jnp.float32)
    selector = selector.reshape(experts * capacity, requests, TOP)
    picker = jnp.sum(selector, axis=-1).astype(jnp.bfloat16)
    outgoing = jnp.dot(picker, normed, preferred_element_type=jnp.float32).astype(jnp.bfloat16)
    outgoing = outgoing.reshape(experts, capacity, normed.shape[1])
    combiner = jnp.sum(selector * gate_vals[None, :, :], axis=-1)
    returned = send_back(
        expert_part(
            lax.all_to_all(outgoing, "req", split_axis=0, concat_axis=0, tiled=True),
            gate_up,
            down_proj,
        )
    )
    moe_sum = jnp.dot(
        combiner.T,
        returned.reshape(experts * capacity, -1),
        precision=lax.Precision.HIGHEST,
        preferred_element_type=jnp.float32,
    )
    moe_share = lax.psum_scatter(moe_sum, "tp", scatter_dimension=1, tiled=True)
    width_here = moe_share.shape[1]
    own_cols = lax.dynamic_slice_in_dim(hidden, tp_place * width_here, width_here, 1)
    return (own_cols.astype(jnp.float32) + moe_share).astype(jnp.bfloat16)


def solution(mesh):
    in_specs = (
        P("req", None),
        P("req", None, "tp"),
        P("req", None, None, "tp"),
        P("req"),
        P("tp", None),
        P(),
        P(),
        P("req", None),
        P("req", None, None, "tp"),
        P("req", "tp", None),
    )
    out_specs = P("req", "tp")
    return jax.shard_map(local, mesh=mesh, in_specs=in_specs, out_specs=out_specs, check_vma=False)
```

profile of v0, /device:TPU:0, one launch (start us, length us, event | category | flops | bytes accessed | tf_op | source)
XLA Modules:
  0.0 238.4 jit_solution(5250030907298059460)
XLA Ops:
  6.5 1.1 convert_bitcast_fusion
  7.7 0.1 fusion.14
  7.9 17.1 %slice_reduce_fusion = (bf16[32,24,1024]{2,1,0:T(8,128)(2,1)}, bf16[32,24,1024]{2,1,0:T(8,128)(2,1)S(1)}) fusion(bf16[32,24,2,1024]{3,2,1,0:T(2,128)(2,1)} %param.12), kind=kLoop, calls=%fused_computation.1 | loop fusion | bytes 6291456 | tf_op jit(solution)/shard_map/slice | solution.py:55
  25.1 0.9 fusion.5
  26.0 0.1 copy.33
  26.3 0.2 copy.38
  26.5 2.0 fusion.2
  28.5 0.1 fusion.13
  28.7 3.8 %fusion.18 = f32[32,2048]{1,0:T(8,128)} fusion(bf16[1024,2048]{1,0:T(8,128)(2,1)} %param.14, bf16[4,8,8,128]{3,2,1,0:T(8,128)(2,1)S(1)} %bitcast.109), kind=kOutput, calls=%fused_computation.36 | convolution fusion | flops 134217728 | bytes 4521984 | tf_op jit(solution)/shard_map/dot_general | solution.py:75
  32.8 0.6 reduce-window.6
  33.4 0.2 slice_reduce_fusion.2
  33.8 0.1 reshape.124
  33.9 19.7 %all-reduce.2.cloned.1.call-done = f32[32,2048]{1,0:T(8,128)} async-done(((f32[32,2048]{1,0:T(8,128)}), f32[32,2048]{1,0:T(8,128)}) %all-reduce.2.cloned.1.call-update) | async-done | bytes 262160 | tf_op jit(solution)/shard_map/psum | solution.py:76
  53.6 1.1 fusion.9
  54.8 0.2 fusion.23
  55.0 2.1 gather_fusion
  57.2 0.1 fusion.33
  57.3 0.2 fusion.30
  57.6 0.4 convert_reduce_fusion
  58.0 2.1 convolution_convert_fusion
  60.0 6.8 %all-to-all-start = ((bf16[16,32,2048]{2,1,0:T(8,128)(2,1)}), bf16[16,32,2048]{2,1,0:T(8,128)(2,1)}, u32[]{:S(2)}, u32[]{:S(2)}) async-start(bf16[16,32,2048]{2,1,0:T(8,128)(2,1)} %bitcast.105), calls=%async_computation | async-start | bytes 4194304 | tf_op jit(solution)/shard_map/all_to_all | solution.py:97
  66.9 0.2 reduce-scatter.2.cloned.1.call-start
  67.1 5.3 %copy.49 = bf16[256,8,2,512]{3,1,2,0:T(8,128)(2,1)} copy(bf16[256,8,2,512]{3,2,1,0:T(2,128)(2,1)} %bitcast.106) | data formatting | bytes 8388608
  72.5 6.5 %copy.30 = bf16[1024,2048]{1,0:T(8,128)(2,1)} copy(bf16[1024,2048]{0,1:T(8,128)(2,1)} %bitcast.104) | data formatting | bytes 8388608 | tf_op jit(solution)/shard_map/dot_general | solution.py:20
  78.9 31.2 %all-to-all-done = bf16[16,32,2048]{2,1,0:T(8,128)(2,1)} async-done(((bf16[16,32,2048]{2,1,0:T(8,128)(2,1)}), bf16[16,32,2048]{2,1,0:T(8,128)(2,1)}, u32[]{:S(2)}, u32[]{:S(2)}) %all-to-all-start) | async-done | bytes 2097184 | tf_op jit(solution)/shard_map/all_to_all | solution.py:97
  110.1 5.2 %fusion.34 = f32[512,2,512]{2,0,1:T(8,128)S(1)} fusion(bf16[512,2048,1]{1,0,2:T(8,128)(2,1)} %bitcast.8, bf16[2,512,2048]{2,1,0:T(8,128)(2,1)} %bitcast.107), kind=kOutput, calls=%fused_computation.68 | convolution fusion | flops 2147483648 | bytes 8388608 | tf_op jit(solution)/shard_map/dot_general | solution.py:20
  115.3 0.3 fusion.8
  115.7 1.3 fusion
  117.0 103.6 %all_to_all.10 = f32[16,32,2048]{2,1,0:T(8,128)S(1)} all-to-all(f32[16,32,2048]{2,1,0:T(8,128)S(1)} %fusion), channel_id=1, replica_groups=mesh['req'=16,'tp'=2] {'req'}, dimensions={0} | all-to-all | bytes 8388608 | tf_op jit(solution)/shard_map/all_to_all | solution.py:30
  220.5 3.2 %fusion.35 = f32[32,2048]{1,0:T(8,128)} fusion(f32[512,32]{0,1:T(8,128)S(1)} %get-tuple-element.8, f32[512,2048]{1,0:T(8,128)S(1)} %bitcast.103), kind=kOutput, calls=%fused_computation.69 | convolution fusion | flops 402653184 | bytes 4521984 | tf_op jit(solution)/shard_map/dot_general | solution.py:102
  223.7 6.3 %reduce-scatter.2.cloned.1.call-done = f32[32,1024]{1,0:T(8,128)} async-done(((f32[32,2048]{1,0:T(8,128)}), f32[32,1024]{1,0:T(8,128)}) %reduce-scatter.2.cloned.1.call-update) | async-done | bytes 131088 | tf_op jit(solution)/shard_map/reduce_scatter | solution.py:108
  230.0 1.6 add_convert_fusion.1
  (41 shorter events, 1.1 us)
Async XLA Ops:
  6.5 109.1 %copy-start = (bf16[1,512,2048]{2,1,0:T(8,128)(2,1)S(1)}, bf16[1,512,2048]{2,1,0:T(8,128)(2,1)}, u32[]{:S(2)}) copy-start(bf16[1,512,2048]{2,1,0:T(8,128)(2,1)} %param.19) | copy-start | bytes 6291460
  6.5 47.1 %all-reduce.2.cloned.1.call-start = ((), (), s32[]{:S(2)}) async-start(), calls=%async_computation.3 | async-start | bytes 524288 | tf_op jit(solution)/shard_map/psum | solution.py:76
  25.1 1.0 copy-start.5
  28.7 3.8 %copy-start.4 = (s32[32,8]{0,1:T(8,128)S(1)}, s32[32,8]{0,1:T(8,128)}, u32[]{:S(2)}) copy-start(s32[32,8]{0,1:T(8,128)} %param.17) | copy-start | bytes 3076
  28.7 25.0 %copy-start.1 = (bf16[32,2048]{1,0:T(8,128)(2,1)S(1)}, bf16[32,2048]{1,0:T(8,128)(2,1)}, u32[]{:S(2)}) copy-start(bf16[32,2048]{1,0:T(8,128)(2,1)} %param.10) | copy-start | bytes 393220
  28.7 26.1 %copy-start.2 = (f32[2048,16]{0,1:T(8,128)S(1)}, f32[2048,16]{0,1:T(8,128)}, u32[]{:S(2)}) copy-start(f32[2048,16]{0,1:T(8,128)} %param.16) | copy-start | bytes 393220
  28.7 26.1 %copy-start.3 = (f32[2048]{0:T(1024)S(1)}, f32[2048]{0:T(1024)}, u32[]{:S(2)}) copy-start(f32[2048]{0:T(1024)} %param.15) | copy-start | bytes 24580
  60.0 50.1 %all-to-all-start = ((bf16[16,32,2048]{2,1,0:T(8,128)(2,1)}), bf16[16,32,2048]{2,1,0:T(8,128)(2,1)}, u32[]{:S(2)}, u32[]{:S(2)}) async-start(bf16[16,32,2048]{2,1,0:T(8,128)(2,1)} %bitcast.105), calls=%async_computation | async-start | bytes 4194304 | tf_op jit(solution)/shard_map/all_to_all | solution.py:97
  66.9 163.1 %reduce-scatter.2.cloned.1.call-start = ((), (), s32[]{:S(2)}) async-start(), calls=%async_computation.4 | async-start | bytes 393216 | tf_op jit(solution)/shard_map/reduce_scatter | solution.py:108
Sparse Core Ops, SparseCore 0:
  32.6 20.9 all-reduce.1
  223.8 6.0 reduce-scatter.1
where the time goes:
time: 239 us; the launch traced here: 238 us
  blocking collectives  104 us (44%)
  waiting for transfers between devices  57.2 us (24%)
  local copies, waits for them, and re-layouts  32.3 us (14%)
  matrix products  18.6 us (8%)
  between operations  13.7 us (6%)
  starting transfers between devices  7.06 us (3%)
  other arithmetic  5.94 us (2%)
    all_to_all x1, blocking collectives, send_back(): lax.all_to_all(results, 'req', split_axis=0, concat_axis=0, tiled=True)  104 us
    all_to_all x1, waiting for transfers between devices, local(): lax.all_to_all(outgoing, 'req', split_axis=0, concat_axis=0, tiled=True)  31.2 us
    psum x1, waiting for transfers between devices, local(): summed = lax.psum(partial_value, 'tp')  19.7 us
    slice x1, local copies, waits for them, and re-layouts, local(): cache_values = kv_cache[:, :, 1].reshape(requests, ctx_len, local_heads, HD)  17.1 us
    all_to_all x1, starting transfers between devices, local(): lax.all_to_all(outgoing, 'req', split_axis=0, concat_axis=0, tiled=True)  6.83 us
    dot_general x1, local copies, waits for them, and re-layouts, expert_part(): jnp.dot(flat_in, gate_up[0].reshape(layout[-1], 2 * units_here), preferre...  6.49 us
    reduce_scatter x1, waiting for transfers between devices, local(): moe_share = lax.psum_scatter(moe_sum, 'tp', scatter_dimension=1, tiled=True)  6.25 us
    unnamed x17, local copies, waits for them, and re-layouts  5.51 us
  transfers between devices with their start and end apart: 3, of which 3 were waited for; matrix products, arithmetic and copies ran while one was open for 6% of the time, Pallas kernels for 0%

commit v1 on v0

--- a/solution.py
+++ b/solution.py
@@ -1,3 +1,4 @@
+import functools
 import jax
 import jax.numpy as jnp
 from jax import lax
@@ -5,6 +6,15 @@
 
 HD = 128
 TOP = 8
+
+
+def play_cells(xs, across):
+    piece_out = lax.all_gather(xs, across)
+    found_now = jnp.sum(piece_out, axis=0)
+    return found_now
+
+
+play_node = functools.partial(play_cells, across="tp")
 
 
 def rms_normed(hidden_in, gain):
@@ -73,7 +83,7 @@
     mixed = mixed + own_weight.astype(jnp.float32)[..., None] * new_values.astype(jnp.float32)
     attended = mixed.astype(jnp.bfloat16).reshape(requests, local_heads * HD)
     partial_value = jnp.dot(attended, out_proj, preferred_element_type=jnp.float32)
-    summed = lax.psum(partial_value, "tp")
+    summed = play_node(partial_value)
     hidden = (residual.astype(jnp.float32) + summed).astype(jnp.bfloat16)
     normed = rms_normed(hidden, norm_gain)
     logits = jnp.dot(normed.astype(jnp.float32), router_weight, precision=lax.Precision.HIGHEST)

time: 239 us -> 222 us (0.929)
  waiting for transfers between devices: 57.2 us -> 37.5 us
    psum x1 -> x0, waiting for transfers between devices: 19.7 us -> none  [local(): summed = lax.psum(partial_value, 'tp')]
    all_gather x0 -> x1, blocking collectives: none -> 2.39 us  [play_cells(): piece_out = lax.all_gather(xs, across)]
    unnamed x17 -> x15, local copies, waits for them, and re-layouts: 5.51 us -> 6.34 us
  transfers between devices with their start and end apart: 3 -> 2, of which waited for: 3 -> 2; matrix products, arithmetic and copies ran while one was open for 6% -> 5% of each run, Pallas kernels for 0% -> 0%
where the time goes in v1:
time: 222 us; the launch traced here: 221 us
  blocking collectives  106 us (48%)
  waiting for transfers between devices  37.5 us (17%)
  local copies, waits for them, and re-layouts  33.1 us (15%)
  matrix products  17.9 us (8%)
  between operations  13.7 us (6%)
  starting transfers between devices  8.51 us (4%)
  other arithmetic  4.88 us (2%)
    all_to_all x1, blocking collectives, send_back(): lax.all_to_all(results, 'req', split_axis=0, concat_axis=0, tiled=True)  103 us
    all_to_all x1, waiting for transfers between devices, local(): lax.all_to_all(outgoing, 'req', split_axis=0, concat_axis=0, tiled=True)  31.3 us
    slice x1, local copies, waits for them, and re-layouts, local(): cache_values = kv_cache[:, :, 1].reshape(requests, ctx_len, local_heads, HD)  17.1 us
    all_to_all x1, starting transfers between devices, local(): lax.all_to_all(outgoing, 'req', split_axis=0, concat_axis=0, tiled=True)  8.29 us
    dot_general x1, local copies, waits for them, and re-layouts, expert_part(): jnp.dot(flat_in, gate_up[0].reshape(layout[-1], 2 * units_here), preferre...  6.49 us
    unnamed x15, local copies, waits for them, and re-layouts  6.34 us
    reduce_scatter x1, waiting for transfers between devices, local(): moe_share = lax.psum_scatter(moe_sum, 'tp', scatter_dimension=1, tiled=True)  6.24 us
    dot_general x1, matrix products, expert_part(): jnp.dot(flat_in, gate_up[0].reshape(layout[-1], 2 * units_here), preferre...  5.19 us
  transfers between devices with their start and end apart: 2, of which 2 were waited for; matrix products, arithmetic and copies ran while one was open for 5% of the time, Pallas kernels for 0%

profile of v1, /device:TPU:0, one launch (start us, length us, event | category | flops | bytes accessed | tf_op | source)
XLA Modules:
  0.0 221.2 jit_solution(3213221975296991410)
XLA Ops:
  6.5 0.9 copy.23
  7.7 0.6 reduce-window.6
  8.2 0.2 slice_reduce_fusion.2
  8.7 0.9 convert_bitcast_fusion
  9.7 0.1 fusion.14
  9.9 17.1 %slice_reduce_fusion = (bf16[32,24,1024]{2,1,0:T(8,128)(2,1)}, bf16[32,24,1024]{2,1,0:T(8,128)(2,1)S(1)}) fusion(bf16[32,24,2,1024]{3,2,1,0:T(2,128)(2,1)} %param.12), kind=kLoop, calls=%fused_computation.1 | loop fusion | bytes 6291456 | tf_op jit(solution)/shard_map/slice | solution.py:65
  27.0 0.9 fusion.5
  28.0 0.1 copy.33
  28.3 0.2 copy.38
  28.5 2.0 fusion.2
  30.5 0.1 fusion.13
  30.7 3.0 %fusion.18 = f32[32,2048]{1,0:T(8,128)S(1)} fusion(bf16[1024,2048]{1,0:T(8,128)(2,1)} %param.14, bf16[4,8,8,128]{3,2,1,0:T(8,128)(2,1)S(1)} %bitcast.111), kind=kOutput, calls=%fused_computation.36 | convolution fusion | flops 134217728 | bytes 4521984 | tf_op jit(solution)/shard_map/dot_general | solution.py:85
  33.7 2.4 %all-gather = f32[64,2048]{1,0:T(8,128)S(1)} all-gather(f32[32,2048]{1,0:T(8,128)S(1)} %fusion.18), channel_id=2, replica_groups=mesh['req'=16,'tp'=2] {'tp'}, dimensions={0}, use_global_device_ids=true | all-gather | bytes 786432 | tf_op jit(solution)/shard_map/all_gather | solution.py:12
  36.2 0.2 fusion.9
  36.4 0.3 fusion.23
  36.7 2.1 gather_fusion
  38.8 0.1 fusion.33
  39.0 0.2 fusion.30
  39.3 0.4 convert_reduce_fusion
  39.7 2.1 convolution_convert_fusion
  41.7 8.3 %all-to-all-start = ((bf16[16,32,2048]{2,1,0:T(8,128)(2,1)}), bf16[16,32,2048]{2,1,0:T(8,128)(2,1)}, u32[]{:S(2)}, u32[]{:S(2)}) async-start(bf16[16,32,2048]{2,1,0:T(8,128)(2,1)} %bitcast.106), calls=%async_computation | async-start | bytes 4194304 | tf_op jit(solution)/shard_map/all_to_all | solution.py:107
  50.0 0.2 reduce-scatter.2.cloned.1.call-start
  50.2 5.3 %copy.49 = bf16[256,8,2,512]{3,1,2,0:T(8,128)(2,1)} copy(bf16[256,8,2,512]{3,2,1,0:T(2,128)(2,1)} %bitcast.107) | data formatting | bytes 8388608
  55.6 6.5 %copy.30 = bf16[1024,2048]{1,0:T(8,128)(2,1)} copy(bf16[1024,2048]{0,1:T(8,128)(2,1)} %bitcast.105) | data formatting | bytes 8388608 | tf_op jit(solution)/shard_map/dot_general | solution.py:30
  62.1 31.3 %all-to-all-done = bf16[16,32,2048]{2,1,0:T(8,128)(2,1)} async-done(((bf16[16,32,2048]{2,1,0:T(8,128)(2,1)}), bf16[16,32,2048]{2,1,0:T(8,128)(2,1)}, u32[]{:S(2)}, u32[]{:S(2)}) %all-to-all-start) | async-done | bytes 2097184 | tf_op jit(solution)/shard_map/all_to_all | solution.py:107
  93.3 5.2 %fusion.34 = f32[512,2,512]{2,0,1:T(8,128)S(1)} fusion(bf16[512,2048,1]{1,0,2:T(8,128)(2,1)} %bitcast.9, bf16[2,512,2048]{2,1,0:T(8,128)(2,1)} %bitcast.108), kind=kOutput, calls=%fused_computation.68 | convolution fusion | flops 2147483648 | bytes 8388608 | tf_op jit(solution)/shard_map/dot_general | solution.py:30
  98.5 0.3 fusion.8
  98.9 1.3 fusion
  100.2 103.2 %all_to_all.10 = f32[16,32,2048]{2,1,0:T(8,128)S(1)} all-to-all(f32[16,32,2048]{2,1,0:T(8,128)S(1)} %fusion), channel_id=1, replica_groups=mesh['req'=16,'tp'=2] {'req'}, dimensions={0} | all-to-all | bytes 8388608 | tf_op jit(solution)/shard_map/all_to_all | solution.py:40
  203.4 3.2 %fusion.35 = f32[32,2048]{1,0:T(8,128)} fusion(f32[512,32]{0,1:T(8,128)S(1)} %get-tuple-element.8, f32[512,2048]{1,0:T(8,128)S(1)} %bitcast.104), kind=kOutput, calls=%fused_computation.69 | convolution fusion | flops 402653184 | bytes 4521984 | tf_op jit(solution)/shard_map/dot_general | solution.py:112
  206.6 6.2 %reduce-scatter.2.cloned.1.call-done = f32[32,1024]{1,0:T(8,128)} async-done(((f32[32,2048]{1,0:T(8,128)}), f32[32,1024]{1,0:T(8,128)}) %reduce-scatter.2.cloned.1.call-update) | async-done | bytes 131088 | tf_op jit(solution)/shard_map/reduce_scatter | solution.py:118
  212.8 1.6 add_convert_fusion.1
  (38 shorter events, 1.1 us)
Async XLA Ops:
  6.5 92.3 %copy-start = (bf16[1,512,2048]{2,1,0:T(8,128)(2,1)S(1)}, bf16[1,512,2048]{2,1,0:T(8,128)(2,1)}, u32[]{:S(2)}) copy-start(bf16[1,512,2048]{2,1,0:T(8,128)(2,1)} %param.19) | copy-start | bytes 6291460
  27.0 1.0 copy-start.4
  30.7 5.5 %copy-start.1 = (bf16[32,2048]{1,0:T(8,128)(2,1)S(1)}, bf16[32,2048]{1,0:T(8,128)(2,1)}, u32[]{:S(2)}) copy-start(bf16[32,2048]{1,0:T(8,128)(2,1)} %param.10) | copy-start | bytes 393220
  33.7 2.7 %copy-start.2 = (f32[2048,16]{0,1:T(8,128)S(1)}, f32[2048,16]{0,1:T(8,128)}, u32[]{:S(2)}) copy-start(f32[2048,16]{0,1:T(8,128)} %param.16) | copy-start | bytes 393220
  33.7 2.7 %copy-start.3 = (f32[2048]{0:T(1024)S(1)}, f32[2048]{0:T(1024)}, u32[]{:S(2)}) copy-start(f32[2048]{0:T(1024)} %param.15) | copy-start | bytes 24580
  41.7 51.6 %all-to-all-start = ((bf16[16,32,2048]{2,1,0:T(8,128)(2,1)}), bf16[16,32,2048]{2,1,0:T(8,128)(2,1)}, u32[]{:S(2)}, u32[]{:S(2)}) async-start(bf16[16,32,2048]{2,1,0:T(8,128)(2,1)} %bitcast.106), calls=%async_computation | async-start | bytes 4194304 | tf_op jit(solution)/shard_map/all_to_all | solution.py:107
  50.0 162.8 %reduce-scatter.2.cloned.1.call-start = ((), (), s32[]{:S(2)}) async-start(), calls=%async_computation.3 | async-start | bytes 393216 | tf_op jit(solution)/shard_map/reduce_scatter | solution.py:118
Sparse Core Ops, SparseCore 0:
  206.7 6.0 reduce-scatter.1
